TPU v7x, 512 devices: a whole 4x4x16 slice. The times are simulated.
512 devices in a mesh: section: 8 (over y, z_hi), dp: 64 (over x, z_lo, core).
Axes of the slice: x: 4, y: 4, z: 16 (z_hi: 2, z_lo: 8; z = z_hi * 8 + z_lo), core: 2. Of those that a mesh axis runs over, the one named last changes fastest.
Arguments:
- first_acts: bfloat16 [4, 8192, 512], P(None, 'dp'), may hold values from -28 to 28
- cotangent: bfloat16 [4, 8192, 512], P(None, 'dp'), may hold values from -28 to 28
- weights: bfloat16 [4096, 512], P(('section', 'dp')), may hold values from -0.25 to 0.25
Outputs:
- update: float32 [4096, 512], P(('section', 'dp'))
All inputs are finite; a program needn't handle non-finite values.
Results may differ from a plain program's by a relative error of at most 0.012.
The roundings to bfloat16 on the way count: a program that leaves them out, or rounds other values in their place, can miss the bound.
Values may be sent and summed in bfloat16 or wider, within the bound.
A program may use at most 64 MiB of HBM per device.

v0:
```python
import jax
import jax.numpy as jnp
from jax import lax
from jax.sharding import PartitionSpec as P


def from_behind(block, axis, distance):
    devices = range(lax.axis_size(axis))
    route = [(i - distance, i) for i in devices if i - distance in devices]
    return lax.ppermute(block, axis, route)


def gelu_parts(h):
    coeff = 0.7978845608028654
    inner = coeff * (h + 0.044715 * h * h * h)
    tanh_val = jnp.tanh(inner)
    value = 0.5 * h * (1.0 + tanh_val)
    slope = 0.5 * (1.0 + tanh_val) + 0.5 * h * (1.0 - tanh_val * tanh_val) * coeff * (
        1.0 + 3.0 * 0.044715 * h * h
    )
    return (value, slope)


def normed(x_val):
    xf = x_val.astype(jnp.float32)
    scale = lax.rsqrt(jnp.mean(xf * xf, axis=-1, keepdims=True) + 1e-05)
    return (xf, scale, (xf * scale).astype(jnp.bfloat16))


def cholesky_apply(factor, rhs):
    half = lax.linalg.triangular_solve(factor, rhs, left_side=True, lower=True)
    return lax.linalg.triangular_solve(factor, half, left_side=True, lower=True, transpose_a=True)


def local(first_acts, cotangent, weights):
    sections = lax.axis_size("section")
    section_id = lax.axis_index("section")
    replicas = lax.axis_size("dp")
    rank = lax.axis_index("dp")
    w_mat = lax.all_gather(weights, "dp", axis=0, tiled=True)
    batches, rows, width = first_acts.shape
    ticks = batches + sections - 1
    count = batches * rows * replicas
    zero_bf = jnp.zeros((rows, width), jnp.bfloat16)
    zero_f = jnp.zeros((rows, width), jnp.float32)

    def forward_tick(carry, tick):
        incoming, saved_x, saved_h = carry
        micro = tick - section_id
        valid = (micro >= 0) & (micro < batches)
        slot = jnp.clip(micro, 0, batches - 1)
        fresh = lax.dynamic_index_in_dim(first_acts, slot, 0, keepdims=False)
        inputs = jnp.where(section_id == 0, fresh, incoming)

        def forward_active(x_val):
            xf, scale, unit = normed(x_val)
            h_val = jnp.dot(unit, w_mat, preferred_element_type=jnp.float32)
            value, slope = gelu_parts(h_val)
            return (h_val, (xf + value).astype(jnp.bfloat16))

        def forward_resting(x_val):
            return (zero_f, zero_bf)

        h_val, outputs = lax.cond(valid, forward_active, forward_resting, inputs)
        old_x = lax.dynamic_index_in_dim(saved_x, slot, 0, keepdims=False)
        old_h = lax.dynamic_index_in_dim(saved_h, slot, 0, keepdims=False)
        saved_x = lax.dynamic_update_index_in_dim(saved_x, jnp.where(valid, inputs, old_x), slot, 0)
        saved_h = lax.dynamic_update_index_in_dim(saved_h, jnp.where(valid, h_val, old_h), slot, 0)
        received = from_behind(outputs, "section", 1)
        return ((received, saved_x, saved_h), None)

    start = (
        zero_bf,
        jnp.zeros((batches, rows, width), jnp.bfloat16),
        jnp.zeros((batches, rows, width), jnp.float32),
    )
    (unused, saved_x, saved_h), empty = lax.scan(forward_tick, start, jnp.arange(ticks))
    zero_sq = jnp.zeros((width, width), jnp.float32)

    def backward_tick(carry, tick):
        incoming, gram_in, gram_out, grad_w = carry
        micro = tick - (sections - 1 - section_id)
        valid = (micro >= 0) & (micro < batches)
        slot = jnp.clip(micro, 0, batches - 1)
        given = lax.dynamic_index_in_dim(cotangent, slot, 0, keepdims=False)
        grad_in = jnp.where(section_id == sections - 1, given, incoming)

        def backward_active(grad_val):
            x_val = lax.dynamic_index_in_dim(saved_x, slot, 0, keepdims=False)
            h_val = lax.dynamic_index_in_dim(saved_h, slot, 0, keepdims=False)
            xf, scale, unit = normed(x_val)
            value, slope = gelu_parts(h_val)
            d_h = (grad_val.astype(jnp.float32) * slope).astype(jnp.bfloat16)
            term_in = jnp.dot(unit.T, unit, preferred_element_type=jnp.float32)
            term_out = jnp.dot(d_h.T, d_h, preferred_element_type=jnp.float32)
            term_w = jnp.dot(unit.T, d_h, preferred_element_type=jnp.float32)
            d_u = jnp.dot(d_h, w_mat.T, preferred_element_type=jnp.float32)
            back = scale * d_u - xf * scale * scale * scale * jnp.mean(
                d_u * xf, axis=-1, keepdims=True
            )
            return (
                (grad_val.astype(jnp.float32) + back).astype(jnp.bfloat16),
                term_in,
                term_out,
                term_w,
            )

        def backward_resting(grad_val):
            return (zero_bf, zero_sq, zero_sq, zero_sq)

        d_x, term_in, term_out, term_w = lax.cond(valid, backward_active, backward_resting, grad_in)
        received = from_behind(d_x, "section", -1)
        return ((received, gram_in + term_in, gram_out + term_out, grad_w + term_w), None)

    begin = (zero_bf, zero_sq, zero_sq, zero_sq)
    (unused, gram_in, gram_out, grad_w), empty = lax.scan(backward_tick, begin, jnp.arange(ticks))
    eye = jnp.eye(width, dtype=jnp.float32)
    share = width // replicas
    total_in, total_out, total_w = lax.psum((gram_in, gram_out, grad_w), "dp")
    chol_in = jnp.linalg.cholesky(total_in / count + 0.1 * eye)
    chol_out = jnp.linalg.cholesky(total_out / count + 0.1 * eye)
    left = cholesky_apply(chol_in, total_w)
    precond = cholesky_apply(chol_out, left.T).T
    scaled = precond / jnp.sqrt(jnp.mean(precond * precond) + 1e-06)
    return lax.dynamic_slice_in_dim(scaled, rank * share, share, 0)


def solution(mesh):
    placed = (P(None, "dp", None), P(None, "dp", None), P(("section", "dp"), None))
    return jax.shard_map(
        local, mesh=mesh, in_specs=placed, out_specs=P(("section", "dp"), None), check_vma=False
    )
```

profile of v0, /device:TPU:1, one launch (start us, length us, event | category | flops | bytes accessed | tf_op | source)
XLA Modules:
  0.0 1771.9 jit_solution(16097294918274121867)
XLA Ops:
  7.2 134.2 %all_gather.3 = bf16[512,512]{1,0:T(8,128)(2,1)} all-gather(bf16[8,512]{1,0:T(8,128)(2,1)S(1)} %copy-done.6), channel_id=1, replica_groups=mesh['section'=8,'dp'=64] {'dp'}, dimensions={0}, use_global_device_ids=true | all-gather | bytes 532480 | tf_op jit(solution)/shard_map/all_gather | solution.py:40
  143.5 230.4 %while.42 = (s32[]{:T(128)}, bf16[128,512]{1,0:T(8,128)(2,1)S(1)}, bf16[4,128,512]{2,1,0:T(8,128)(2,1)}, f32[4,128,512]{2,1,0:T(8,128)}, s32[11]{0:T(128)S(1)}, ...) while((s32[]{:T(128)}, bf16[128,512]{1,0:T(8,128)(2,1)S(1)}, ...), condition=%wide.region_4.5_spmd, body=%wide.region_0.4_spmd.sunk | while | flops 68419720 | bytes 3935009 | solution.py:77
  148.7 6.5 collective-permute-start
  157.0 3.3 collective-permute-done
  165.5 12.8 collective-permute-start
  186.9 12.8 collective-permute-start
  208.6 12.8 collective-permute-start
  229.0 14.3 collective-permute-start
  250.8 12.8 collective-permute-start
  265.3 3.0 collective-permute-done
  272.1 12.8 collective-permute-start
  293.0 12.8 collective-permute-start
  313.8 12.8 collective-permute-start
  334.6 12.8 collective-permute-start
  355.5 12.8 collective-permute-start
  370.1 3.8 collective-permute-done
  373.9 235.7 %while.43 = (s32[]{:T(128)}, bf16[128,512]{1,0:T(8,128)(2,1)S(1)}, f32[512,512]{1,0:T(8,128)}, f32[512,512]{1,0:T(8,128)}, f32[512,512]{1,0:T(8,128)}, /*index=5...) while((s32[]{:T(128)}, bf16[128,512]{1,0:T(8,128)(2,1)S(1)}, ...), condition=%wide.region_10.11_spmd.clone, body=%wide.region_5.10_spmd.clone.sunk | while | flops 272826496 | bytes 16127352 | solution.py:116
  380.0 11.3 collective-permute-done.1
  394.2 3.4 select_add_fusion.8
  400.1 7.6 collective-permute-done.1
  410.7 3.4 select_add_fusion.8
  416.5 10.8 collective-permute-done.1
  430.3 3.4 select_add_fusion.8
  436.1 12.3 collective-permute-done.1
  451.4 3.4 select_add_fusion.8
  457.3 9.5 collective-permute-done.1
  469.7 3.4 select_add_fusion.8
  475.6 8.0 collective-permute-done.1
  486.5 3.4 select_add_fusion.8
  492.4 20.1 %collective-permute-done.1 = bf16[128,512]{1,0:T(8,128)(2,1)S(1)} collective-permute-done((bf16[128,512]{1,0:T(8,128)(2,1)S(1)}, bf16[128,512]{1,0:T(8,128)(2,1)S(1)}, u32[]{:S(2)}, u32[]{:S(2)}) %collective-permute-start.1) | collective-permute-done | bytes 131104 | tf_op jit(solution)/shard_map/while/body/eval_jaxpr/ppermute | solution.py:10
  513.7 6.8 conditional.6
  521.8 3.4 select_add_fusion.8
  527.7 9.7 collective-permute-done.1
  538.6 6.8 conditional.6
  546.7 3.4 select_add_fusion.8
  552.6 9.5 collective-permute-done.1
  563.3 6.8 conditional.6
  571.4 3.4 select_add_fusion.8
  577.2 9.5 collective-permute-done.1
  587.9 6.8 conditional.6
  596.0 3.4 select_add_fusion.8
  601.9 7.3 collective-permute-done.1
  609.6 2.5 copy.4
  612.1 2.6 copy.6
  614.8 854.0 %all-reduce.4.cloned.1.call-done = (f32[512,512]{1,0:T(8,128)}, f32[512,512]{0,1:T(8,128)}, f32[512,512]{0,1:T(8,128)}) async-done(((f32[512,512]{1,0:T(8,128)}, f32[512,512]{0,1:T(8,128)}, f32[512,512]{0,1:T(8,128)}), (f32[512,512]{1,0:T(8,128)}, f32[512,512]{0,1:T(8,128)}, f32[512,512]{0,1:T(8,128)})) %all-reduce.4.cloned.1.call-update) | async-done | bytes 3145744 | tf_op jit(solution)/shard_map/psum | solution.py:119
  1468.8 2.8 select_add_fusion.3
  1473.1 11.7 cholesky.286
  1484.9 9.8 custom-call.34
  1495.4 11.7 cholesky.305
  1508.4 10.0 custom-call.35
  1519.1 11.7 cholesky.326
  1531.5 9.8 custom-call.36
  1542.0 12.1 cholesky.343
  1557.3 7.5 while.45
  1564.8 39.3 %custom-call.43 = f32[4,128,128]{1,2,0:T(8,128)S(1)} custom-call(f32[4,128,128]{2,1,0:T(8,128)S(1)} %get-tuple-element.391), custom_call_target="InvertDiagBlocksLowerTriangular" | custom-call | tf_op jit(solution)/shard_map/triangular_solve/custom-call.8 | solution.py:32
  1607.1 11.7 cholesky.358
  1619.0 9.8 custom-call.37
  1630.2 11.7 cholesky.377
  1643.3 9.9 custom-call.38
  1655.4 13.2 cholesky.398
  1670.7 11.3 custom-call.39
  1683.4 11.7 cholesky.415
  1698.5 8.1 while.44
  1706.7 39.5 %custom-call.41 = f32[4,128,128]{1,2,0:T(8,128)S(1)} custom-call(f32[4,128,128]{2,1,0:T(8,128)S(1)} %get-tuple-element.389), custom_call_target="InvertDiagBlocksLowerTriangular" | custom-call | tf_op jit(solution)/shard_map/triangular_solve/custom-call.8 | solution.py:32
  (324 shorter events, 219.1 us)
Async XLA Ops:
  6.5 1462.2 %all-reduce.4.cloned.1.call-start = ((), (), s32[]{:S(2)}) async-start(), calls=%async_computation | async-start | bytes 6291456 | tf_op jit(solution)/shard_map/psum | solution.py:119
  6.5 0.7 copy-start.6
  148.7 11.5 collective-permute-start
  165.5 16.2 collective-permute-start
  186.9 16.5 collective-permute-start
  208.6 16.6 collective-permute-start
  229.0 18.1 %collective-permute-start = (bf16[128,512]{1,0:T(8,128)(2,1)S(1)}, bf16[128,512]{1,0:T(8,128)(2,1)S(1)}, u32[]{:S(2)}, u32[]{:S(2)}) collective-permute-start(bf16[128,512]{1,0:T(8,128)(2,1)S(1)} %get-tuple-element.669), channel_id=1, source_target_pairs={{0,64},{64,128},{128,192},{192,256},{256,320},{320,384},{384,448},... | collective-permute-start | bytes 393224 | tf_op jit(solution)/shard_map/while/body/eval_jaxpr/ppermute | solution.py:10
  250.8 17.6 collective-permute-start
  272.1 17.1 collective-permute-start
  293.0 17.1 collective-permute-start
  313.8 17.1 collective-permute-start
  334.6 17.1 collective-permute-start
  355.5 18.4 %collective-permute-start = (bf16[128,512]{1,0:T(8,128)(2,1)S(1)}, bf16[128,512]{1,0:T(8,128)(2,1)S(1)}, u32[]{:S(2)}, u32[]{:S(2)}) collective-permute-start(bf16[128,512]{1,0:T(8,128)(2,1)S(1)} %get-tuple-element.669), channel_id=1, source_target_pairs={{0,64},{64,128},{128,192},{192,256},{256,320},{320,384},{384,448},... | collective-permute-start | bytes 393224 | tf_op jit(solution)/shard_map/while/body/eval_jaxpr/ppermute | solution.py:10
  375.6 15.7 collective-permute-start.1
  392.9 14.8 collective-permute-start.1
  409.3 18.0 %collective-permute-start.1 = (bf16[128,512]{1,0:T(8,128)(2,1)S(1)}, bf16[128,512]{1,0:T(8,128)(2,1)S(1)}, u32[]{:S(2)}, u32[]{:S(2)}) collective-permute-start(bf16[128,512]{1,0:T(8,128)(2,1)S(1)} %get-tuple-element.684), channel_id=1, source_target_pairs={{64,0},{128,64},{192,128},{256,192},{320,256},{384,320},{448,384},... | collective-permute-start | bytes 393224 | tf_op jit(solution)/shard_map/while/body/eval_jaxpr/ppermute | solution.py:10
  429.0 19.5 %collective-permute-start.1 = (bf16[128,512]{1,0:T(8,128)(2,1)S(1)}, bf16[128,512]{1,0:T(8,128)(2,1)S(1)}, u32[]{:S(2)}, u32[]{:S(2)}) collective-permute-start(bf16[128,512]{1,0:T(8,128)(2,1)S(1)} %get-tuple-element.684), channel_id=1, source_target_pairs={{64,0},{128,64},{192,128},{256,192},{320,256},{384,320},{448,384},... | collective-permute-start | bytes 393224 | tf_op jit(solution)/shard_map/while/body/eval_jaxpr/ppermute | solution.py:10
  450.1 16.7 collective-permute-start.1
  468.4 15.1 collective-permute-start.1
  485.2 27.3 %collective-permute-start.1 = (bf16[128,512]{1,0:T(8,128)(2,1)S(1)}, bf16[128,512]{1,0:T(8,128)(2,1)S(1)}, u32[]{:S(2)}, u32[]{:S(2)}) collective-permute-start(bf16[128,512]{1,0:T(8,128)(2,1)S(1)} %get-tuple-element.684), channel_id=1, source_target_pairs={{64,0},{128,64},{192,128},{256,192},{320,256},{384,320},{448,384},... | collective-permute-start | bytes 393224 | tf_op jit(solution)/shard_map/while/body/eval_jaxpr/ppermute | solution.py:10
  520.5 16.8 collective-permute-start.1
  545.4 16.6 collective-permute-start.1
  570.1 16.6 collective-permute-start.1
  594.7 14.4 collective-permute-start.1
  1471.6 1.2 copy-start.1
  1604.2 1.7 copy-start
  1606.1 1.0 copy-start.2
  1607.1 21.7 %copy-start.3 = (f32[512,512]{1,0:T(8,128)S(1)}, f32[512,512]{1,0:T(8,128)}, u32[]{:S(2)}) copy-start(f32[512,512]{1,0:T(8,128)} %copy-done.2) | copy-start | bytes 3145732
  1629.5 0.7 copy-start.5
  1746.2 3.2 copy-start.4
Sparse Core Ops, SparseCore 0:
  614.9 853.8 all-reduce.3
where the time goes:
time: 1780 us; the launch traced here: 1770 us
  waiting for transfers between devices  997 us (56%)
  other arithmetic  344 us (19%)
  starting transfers between devices  150 us (8%)
  blocking collectives  134 us (8%)
  local copies, waits for them, and re-layouts  66.3 us (4%)
  matrix products  44.7 us (3%)
  between operations  19.8 us (1%)
    psum x1, waiting for transfers between devices, local(): total_in, total_out, total_w = lax.psum((gram_in, gram_out, grad_w), 'dp')  854 us
    ppermute x22, starting transfers between devices, from_behind(): return lax.ppermute(block, axis, route)  150 us
    ppermute x22, waiting for transfers between devices, from_behind(): return lax.ppermute(block, axis, route)  143 us
    all_gather x1, blocking collectives, local(): w_mat = lax.all_gather(weights, 'dp', axis=0, tiled=True)  134 us
    another operation x15, other arithmetic, local(): chol_in = jnp.linalg.cholesky(total_in / count + 0.1 * eye)  83.6 us
    another operation x15, other arithmetic, local(): chol_out = jnp.linalg.cholesky(total_out / count + 0.1 * eye)  79.6 us
    another operation x5, other arithmetic, cholesky_apply(): lax.linalg.triangular_solve(factor, half, left_side=True, lower=True, tra...  79.1 us
    add x11, other arithmetic, backward_tick(): grad_w + term_w  36 us
  transfers between devices with their start and end apart: 23, of which 23 were waited for; matrix products, arithmetic and copies ran while one was open for 5% of the time, Pallas kernels for 0%

commit v1 on v0

v1 whole, which is shorter than its diff:
```python
import jax
import jax.numpy as jnp
from jax import lax
from jax.experimental import pallas as pl
from jax.experimental.pallas import tpu as pltpu
from jax.sharding import PartitionSpec as P

MESH = pl.DeviceIdType.MESH
HIGHEST = lax.Precision.HIGHEST
WIDTH = 512
TOKENS = 512
LAYERS = 8
CHUNKS = 128
ROWS = 40
VMEM_LIMIT = 56 * 1024 * 1024


def place():
    section = lax.axis_index("section")
    rank = lax.axis_index("dp")
    y, z_hi = section // 2, section % 2
    x, z_lo, core = rank // 16, (rank % 16) // 2, rank % 2
    return x, y, z_hi, z_lo, core


def device(x, y, z_hi, z_lo, core):
    return (y * 2 + z_hi, x * 16 + z_lo * 2 + core)


def flip_low(v):
    return v + 1 - 2 * (v % 2)


def send(src, dst, send_sem, recv_sem, target):
    copy = pltpu.make_async_remote_copy(
        src_ref=src, dst_ref=dst, send_sem=send_sem, recv_sem=recv_sem,
        device_id=target, device_id_type=MESH,
    )
    copy.start()
    return copy


def meet(targets):
    barrier = pltpu.get_barrier_semaphore()
    for target in targets:
        pl.semaphore_signal(barrier, inc=1, device_id=target, device_id_type=MESH)
    pl.semaphore_wait(barrier, len(targets))


def gather_kernel(w_ref, buf, mine_ref, sib_ref, sib_sem, z_send, z_recv, h_send, h_recv, c_send, c_recv):
    x, y, z_hi, z_lo, core = place()
    z = z_hi * 8 + z_lo
    sibling = device(x, y, z_hi, z_lo, 1 - core)
    z_peers = []
    for k in range(1, 16):
        other = (z + k) % 16
        z_peers.append(device(x, y, other // 8, other % 8, core))
    moves = [
        (lambda a, b: (flip_low(a), b)),
        (lambda a, b: (3 - a, b)),
        (lambda a, b: (a, flip_low(b))),
        (lambda a, b: (a, 3 - b)),
    ]
    orders = [(0, 1, 2, 3), (1, 2, 3, 0), (2, 3, 0, 1), (3, 0, 1, 2)]
    partners = []
    for move in moves:
        px, py = move(x, y)
        partners.append(device(px, py, z_hi, z_lo, core))
    meet([sibling] + z_peers + partners)

    first = core == 0
    wf = w_ref[...].astype(jnp.float32)
    left, right = wf[:, :256], wf[:, 256:]
    mine_ref[...] = jnp.where(first, right, left)
    swap = send(mine_ref, sib_ref, sib_sem.at[0], sib_sem.at[1], sibling)
    mine = jnp.where(first, left, right)
    swap.wait()
    theirs = sib_ref[...]
    rows = jnp.concatenate([jnp.where(first, mine, theirs), jnp.where(first, theirs, mine)], axis=0)
    own = buf.at[core, y, z_hi, x, pl.ds(pl.multiple_of(z_lo * 16, 16), 16), :]
    own[...] = rows.astype(jnp.bfloat16)
    z_copies = [send(own, own, z_send.at[k], z_recv.at[k], z_peers[k - 1]) for k in range(1, 16)]
    for copy in z_copies:
        copy.wait_recv()

    def block(j, at):
        bx, by = at
        return buf.at[core, by, j // 2, bx, pl.ds((j % 2) * 64, 64), :]

    held = {}
    copies = {}
    across = {}

    def forward(j, r, step_from):
        ref = block(j, held[j, r])
        for step in range(step_from, 4):
            index = 2 ** step + r
            copies[j, index] = send(
                ref, ref, h_send.at[j, index], h_recv.at[j, index], partners[orders[j][step]]
            )
        across[j, r] = send(ref, ref, c_send.at[j, r], c_recv.at[j, r], sibling)

    for j in range(4):
        held[j, 0] = (x, y)
        for r in range(1, 16):
            step = r.bit_length() - 1
            held[j, r] = moves[orders[j][step]](*held[j, r - 2 ** step])
    for j in range(4):
        forward(j, 0, 0)
    arrivals = sorted(range(1, 16), key=lambda r: (bin(r).count("1"), r))
    for r in arrivals:
        for j in range(4):
            copies[j, r].wait_recv()
            forward(j, r, r.bit_length())
    for j in range(4):
        for r in range(16):
            across[j, r].wait_recv()
    for copy in z_copies:
        copy.wait_send()
    for j in range(4):
        for r in range(16):
            across[j, r].wait_send()
            if r:
                copies[j, r].wait_send()


def gather(weights):
    return pl.pallas_call(
        gather_kernel,
        out_shape=jax.ShapeDtypeStruct((2, 4, 2, 4, 128, 256), jnp.bfloat16),
        in_specs=[pl.BlockSpec(memory_space=pltpu.VMEM)],
        out_specs=pl.BlockSpec(memory_space=pltpu.VMEM),
        scratch_shapes=[
            pltpu.VMEM((8, 256), jnp.float32),
            pltpu.VMEM((8, 256), jnp.float32),
            pltpu.SemaphoreType.DMA((2,)),
            pltpu.SemaphoreType.DMA((16,)),
            pltpu.SemaphoreType.DMA((16,)),
            pltpu.SemaphoreType.DMA((4, 16)),
            pltpu.SemaphoreType.DMA((4, 16)),
            pltpu.SemaphoreType.DMA((4, 16)),
            pltpu.SemaphoreType.DMA((4, 16)),
        ],
        compiler_params=pltpu.CompilerParams(
            collective_id=0, has_side_effects=True, vmem_limit_bytes=VMEM_LIMIT
        ),
        name="weights_gather",
    )(weights)


def gelu_parts(h):
    coeff = 0.7978845608028654
    inner = coeff * (h + 0.044715 * h * h * h)
    tanh_val = jnp.tanh(inner)
    value = 0.5 * h * (1.0 + tanh_val)
    slope = 0.5 * (1.0 + tanh_val) + 0.5 * h * (1.0 - tanh_val * tanh_val) * coeff * (
        1.0 + 3.0 * 0.044715 * h * h
    )
    return (value, slope)


def dot(a, b, dims, precision=None):
    return lax.dot_general(
        a, b, ((dims[:1], dims[1:]), ((), ())), precision=precision,
        preferred_element_type=jnp.float32,
    )


SPLIT = 128


def chain_kernel(act_ref, cot_ref, w_ref, out_ref, xs, slopes, scales, grads, u_own, dh_own):
    section = lax.axis_index("section")
    parts = TOKENS // SPLIT
    xs[0] = act_ref[...]
    grads[...] = cot_ref[...]

    def ahead(layer, carry):
        for part in range(parts):
            rows = pl.ds(part * SPLIT, SPLIT)
            xf = xs[layer, rows, :].astype(jnp.float32)
            scale = lax.rsqrt(jnp.mean(xf * xf, axis=-1, keepdims=True) + 1e-05)
            scales[layer, rows, :] = jnp.broadcast_to(scale, (SPLIT, 128))
            unit = (xf * scale).astype(jnp.bfloat16)

            @pl.when(layer == section)
            def _():
                u_own[rows, :] = unit

            for half in range(2):
                columns = pl.ds(half * 256, 256)
                h_val = dot(unit, w_ref[half, layer], (1, 0))
                value, slope = gelu_parts(h_val)
                slopes[layer, rows, columns] = slope
                xs[layer + 1, rows, columns] = (xf[:, half * 256:half * 256 + 256] + value).astype(jnp.bfloat16)
        return carry

    lax.fori_loop(0, LAYERS, ahead, 0)

    def back(step, carry):
        layer = LAYERS - 1 - step
        for part in range(parts):
            rows = pl.ds(part * SPLIT, SPLIT)
            grad = grads[rows, :].astype(jnp.float32)
            d_h = (grad * slopes[layer, rows, :]).astype(jnp.bfloat16)

            @pl.when(layer == section)
            def _():
                dh_own[rows, :] = d_h

            d_u = dot(d_h[:, :256], w_ref[0, layer], (1, 1)) + dot(d_h[:, 256:], w_ref[1, layer], (1, 1))
            xf = xs[layer, rows, :].astype(jnp.float32)
            scale = scales[layer, rows, 0:1]
            shift = scale * scale * scale * jnp.mean(d_u * xf, axis=-1, keepdims=True)
            grads[rows, :] = (grad + (scale * d_u - xf * shift)).astype(jnp.bfloat16)
        return carry

    lax.fori_loop(0, LAYERS, back, 0)

    def keep(at, value):
        for half in range(value.shape[1] // 128):
            out_ref[at + half] = value[:, half * 128:half * 128 + 128]

    for base, ref in ((0, u_own), (6, dh_own)):
        for at, low, high in ((0, 0, 0), (2, 256, 0), (4, 256, 256)):
            keep(base + at, dot(ref[:, low:low + 256], ref[:, high:high + 256], (0, 0)))
    for top in range(2):
        keep(12 + 4 * top, dot(u_own[:, top * 256:top * 256 + 256], dh_own[...], (0, 0)))


def chain(acts, cots, w_all):
    return pl.pallas_call(
        chain_kernel,
        out_shape=jax.ShapeDtypeStruct((20, 256, 128), jnp.float32),
        in_specs=[pl.BlockSpec(memory_space=pltpu.VMEM)] * 3,
        out_specs=pl.BlockSpec(memory_space=pltpu.VMEM),
        scratch_shapes=[
            pltpu.VMEM((LAYERS + 1, TOKENS, WIDTH), jnp.bfloat16),
            pltpu.VMEM((LAYERS, TOKENS, WIDTH), jnp.float32),
            pltpu.VMEM((LAYERS, TOKENS, 128), jnp.float32),
            pltpu.VMEM((TOKENS, WIDTH), jnp.bfloat16),
            pltpu.VMEM((TOKENS, WIDTH), jnp.bfloat16),
            pltpu.VMEM((TOKENS, WIDTH), jnp.bfloat16),
        ],
        compiler_params=pltpu.CompilerParams(vmem_limit_bytes=VMEM_LIMIT),
        name="layer_chain",
    )(acts, cots, w_all)


def reduce_kernel(part_ref, out_ref, acc, got_core, got_x1, got_x2, got_z1, got_z2, got_z4, sems):
    x, y, z_hi, z_lo, core = place()
    x_low, x_high = ((x + 1) // 2) % 2, x // 2
    z_bits = (z_lo % 2, (z_lo // 2) % 2, z_lo // 4)
    sibling = device(x, y, z_hi, z_lo, 1 - core)
    x_low_peer = device(flip_low(x), y, z_hi, z_lo, core)
    x_high_peer = device(3 - x, y, z_hi, z_lo, core)
    z_peers = []
    for bit, distance in zip(z_bits, (1, 2, 4)):
        z_peers.append(device(x, y, z_hi, z_lo + distance * (1 - 2 * bit), core))
    meet([sibling, x_low_peer, x_high_peer] + z_peers)

    copies = []

    def move(step, sub, src, dst, target):
        copy = send(src, dst, sems.at[0, step, sub], sems.at[1, step, sub], target)
        copies.append(copy)
        return copy

    swap = move(0, 0, part_ref.at[pl.ds((1 - core) * 64, 64)], got_core, sibling)
    swap.wait_recv()
    acc[...] = part_ref[pl.ds(core * 64, 64)] + got_core[...]

    order = [
        [(x_low, x_low_peer), (x_high, x_high_peer)],
        [(x_high, x_high_peer), (x_low, x_low_peer)],
    ]
    for sub in range(2):
        order[sub] += list(zip(z_bits, z_peers))
    base = [0, 32]
    for step in range(5):
        size = 16 >> step
        got = (got_x1, got_x2, got_z1, got_z2, got_z4)[step]
        waits = []
        for sub in range(2):
            bit, peer = order[sub][step]
            waits.append(move(1 + step, sub, acc.at[pl.ds(base[sub] + (1 - bit) * size, size)], got.at[sub], peer))
            base[sub] = base[sub] + bit * size
        for sub in range(2):
            waits[sub].wait_recv()
            mine = pl.ds(base[sub], size)
            acc[mine] = acc[mine] + got[sub]
    final = [core * 64 + base[sub] for sub in range(2)]
    for sub in range(2):
        out_ref[pl.ds(final[sub], 1)] = acc[pl.ds(base[sub], 1)]
    for step in reversed(range(5)):
        size = 16 >> step
        waits = []
        for sub in range(2):
            bit, peer = order[sub][step]
            mine = out_ref.at[pl.ds(final[sub], size)]
            waits.append(move(6 + step, sub, mine, mine, peer))
            final[sub] = final[sub] - bit * size
        for sub in range(2):
            waits[sub].wait_recv()
    waits = []
    for sub in range(2):
        mine = out_ref.at[pl.ds(core * 64 + sub * 32, 32)]
        waits.append(move(11, sub, mine, mine, sibling))
    for sub in range(2):
        waits[sub].wait_recv()
    for copy in copies:
        copy.wait_send()


def reduce_all(partial):
    chunk = lambda *lead: pltpu.VMEM(lead + (ROWS, 128), jnp.float32)
    return pl.pallas_call(
        reduce_kernel,
        out_shape=jax.ShapeDtypeStruct((CHUNKS, ROWS, 128), jnp.float32),
        in_specs=[pl.BlockSpec(memory_space=pltpu.VMEM)],
        out_specs=pl.BlockSpec(memory_space=pltpu.VMEM),
        scratch_shapes=[
            chunk(64), chunk(64), chunk(2, 16), chunk(2, 8), chunk(2, 4), chunk(2, 2), chunk(2, 1),
            pltpu.SemaphoreType.DMA((2, 12, 2)),
        ],
        compiler_params=pltpu.CompilerParams(
            collective_id=1, has_side_effects=True, vmem_limit_bytes=VMEM_LIMIT
        ),
        name="sums_reduce",
    )(partial)


def splat(value):
    return jnp.broadcast_to(value, (8, 128))


def panel_step(tiles):
    pivot = tiles[0]
    lane = lax.broadcasted_iota(jnp.int32, (8, 128), 1)
    row = lax.broadcasted_iota(jnp.int32, (8, 128), 0)
    columns = [splat(pivot[:, k:k + 1]) for k in range(8)]
    e = {}
    for k in range(8):
        for i in range(k + 1):
            e[i, k] = splat(columns[k][i:i + 1, :])
    at = lambda i, k: (min(i, k), max(i, k))
    for k in range(8):
        inverse = 1.0 / e[k, k]
        scaled = {i: e[at(i, k)] * inverse for i in range(8) if i != k}
        for i in range(8):
            for j in range(i, 8):
                if i != k and j != k:
                    e[i, j] = e[i, j] - e[at(i, k)] * scaled[j]
        for i in scaled:
            e[at(i, k)] = scaled[i]
        e[k, k] = -inverse
    in_block = lane < 8
    top = jnp.where(in_block, jnp.where(lane == row, 1.0, 0.0), pivot)
    result = None
    for k in range(8):
        column = e[at(0, k)]
        for i in range(1, 8):
            column = jnp.where(row == i, e[at(i, k)], column)
        term = column * splat(top[k:k + 1, :])
        result = -term if result is None else result - term
    spread = [splat(result[k:k + 1, :]) for k in range(8)]
    moved = []
    for tile in tiles[1:]:
        value = jnp.where(in_block, 0.0, tile)
        for k in range(8):
            value = value - splat(tile[:, k:k + 1]) * spread[k]
        moved.append(value)
    moved.append(result)
    return [pltpu.roll(tile, 120, 1) for tile in moved]


def solve_kernel(sum_ref, out_ref, mats, d_mat, p_mat):
    rank = lax.axis_index("dp")
    row = lax.broadcasted_iota(jnp.int32, (WIDTH, WIDTH), 0)
    lane = lax.broadcasted_iota(jnp.int32, (WIDTH, WIDTH), 1)
    shift = jnp.where(row == lane, 0.1, 0.0)
    for which in range(2):
        base = 6 * which
        for half in range(2):
            columns = slice(half * 128, half * 128 + 128)
            mats[which, :256, columns] = sum_ref[base + half]
            mats[which, 256:, columns] = sum_ref[base + 2 + half]
            mats[which, columns, 256:] = sum_ref[base + 2 + half].T
            mats[which, 256:, 256 + half * 128:384 + half * 128] = sum_ref[base + 4 + half]
        mats[which] = mats[which] * (1.0 / 32768.0) + shift
    for top in range(2):
        for quarter in range(4):
            d_mat[top * 256:top * 256 + 256, quarter * 128:quarter * 128 + 128] = sum_ref[12 + 4 * top + quarter]

    block_row = lax.broadcasted_iota(jnp.int32, (128, 128), 0)
    block_lane = lax.broadcasted_iota(jnp.int32, (128, 128), 1)
    unit = jnp.where(block_row == block_lane, 1.0, 0.0)
    for k in range(4):
        span = slice(k * 128, k * 128 + 128)
        start = []
        for which in range(2):
            for i in range(16):
                start.append(mats[which, k * 128 + i * 8:k * 128 + i * 8 + 8, span])

        def advance(step, tiles):
            return tuple(panel_step(list(tiles[:16])) + panel_step(list(tiles[16:])))

        done = lax.fori_loop(0, 16, advance, tuple(start))
        for which in range(2):
            inverse = jnp.concatenate(done[16 * which:16 * which + 16], axis=0)
            side = mats[which, :, span]
            mats[which, :, span] = jnp.zeros((WIDTH, 128), jnp.float32)
            mats[which, span, span] = unit
            top = dot(inverse, mats[which, span, :], (1, 0), HIGHEST)
            for i in range(4):
                here = slice(i * 128, i * 128 + 128)
                if i == k:
                    mats[which, here, :] = top
                else:
                    mats[which, here, :] = mats[which, here, :] - dot(side[here], top, (1, 0), HIGHEST)
    p_mat[...] = dot(mats[0], d_mat[...], (1, 0), HIGHEST)
    p_mat[...] = dot(p_mat[...], mats[1], (1, 0), HIGHEST)
    whole = p_mat[...]
    mean = jnp.sum(jnp.sum(whole * whole, axis=0, keepdims=True), axis=1, keepdims=True) * (1.0 / (WIDTH * WIDTH))
    mine = p_mat[pl.ds(pl.multiple_of(rank * 8, 8), 8), :]
    out_ref[...] = mine / jnp.sqrt(mean + 1e-06)


def solve(sums):
    square = pltpu.VMEM((WIDTH, WIDTH), jnp.float32)
    return pl.pallas_call(
        solve_kernel,
        out_shape=jax.ShapeDtypeStruct((8, WIDTH), jnp.float32),
        in_specs=[pl.BlockSpec(memory_space=pltpu.VMEM)],
        out_specs=pl.BlockSpec(memory_space=pltpu.VMEM),
        scratch_shapes=[pltpu.VMEM((2, WIDTH, WIDTH), jnp.float32), square, square],
        compiler_params=pltpu.CompilerParams(vmem_limit_bytes=VMEM_LIMIT),
        name="factor_solve",
    )(sums)


def local(first_acts, cotangent, weights):
    w_all = gather(weights).reshape(2, LAYERS, WIDTH, 256)
    partial = chain(first_acts.reshape(TOKENS, WIDTH), cotangent.reshape(TOKENS, WIDTH), w_all)
    sums = reduce_all(partial.reshape(CHUNKS, ROWS, 128)).reshape(20, 256, 128)
    return solve(sums)


def solution(mesh):
    placed = (P(None, "dp", None), P(None, "dp", None), P(("section", "dp"), None))
    return jax.shard_map(
        local, mesh=mesh, in_specs=placed, out_specs=P(("section", "dp"), None), check_vma=False
    )
```

time: 1780 us -> 218 us (0.12)
  the two profiles are of different devices: /device:TPU:1 before, /device:TPU:8 now
where the time goes in v1:
time: 218 us; the launch traced here: 217 us
  Pallas kernels  217 us (100%)
    pallas_call x1, Pallas kernels, reduce_all(): pl.pallas_call(reduce_kernel, out_shape=jax.ShapeDtypeStruct((CHUNKS, ROW...  73 us
    pallas_call x1, Pallas kernels, solve(): pl.pallas_call(solve_kernel, out_shape=jax.ShapeDtypeStruct((8, WIDTH), j...  62.3 us
    pallas_call x1, Pallas kernels, gather(): pl.pallas_call(gather_kernel, out_shape=jax.ShapeDtypeStruct((2, 4, 2, 4,...  46.9 us
    pallas_call x1, Pallas kernels, chain(): pl.pallas_call(chain_kernel, out_shape=jax.ShapeDtypeStruct((20, 256, 128...  35 us

profile of v1, /device:TPU:8, one launch (start us, length us, event | category | flops | bytes accessed | tf_op | source)
XLA Modules:
  0.0 217.2 jit_solution(8857747131956144426)
XLA Ops:
  0.0 46.9 %weights_gather.1 = bf16[2,4,2,4,128,256]{5,4,3,2,1,0:T(8,128)(2,1)} custom-call(bf16[8,512]{1,0:T(8,128)(2,1)} %w_ref.1), custom_call_target="tpu_custom_call" | custom-call | tf_op jit(solution)/shard_map/weights_gather/pallas_call | solution.py:128
  46.9 35.0 %layer_chain.1 = f32[20,256,128]{2,1,0:T(8,128)} custom-call(bf16[512,512]{1,0:T(8,128)(2,1)} %bitcast.8, bf16[512,512]{1,0:T(8,128)(2,1)} %bitcast.9, bf16[2,8,512,256]{3,2,1,0:T(8,128)(2,1)} %bitcast.5), custom_call_target="tpu_custom_call" | custom-call | tf_op jit(solution)/shard_map/layer_chain/pallas_call | solution.py:232
  82.0 73.0 %sums_reduce.1 = f32[128,40,128]{2,1,0:T(8,128)} custom-call(f32[128,40,128]{2,1,0:T(8,128)} %bitcast.7), custom_call_target="tpu_custom_call" | custom-call | tf_op jit(solution)/shard_map/sums_reduce/pallas_call | solution.py:317
  154.9 62.3 %factor_solve.1 = f32[8,512]{1,0:T(8,128)} custom-call(f32[20,256,128]{2,1,0:T(8,128)} %bitcast.6), custom_call_target="tpu_custom_call" | custom-call | tf_op jit(solution)/shard_map/factor_solve/pallas_call | solution.py:431

commit v2 on v0

v2 whole, which is shorter than its diff:
```python
import functools

import jax
import jax.numpy as jnp
from jax import lax
from jax.experimental import pallas as pl
from jax.experimental.pallas import tpu as pltpu
from jax.sharding import PartitionSpec as P

MESH = pl.DeviceIdType.MESH
WIDTH = 512
TOKENS = 512
LAYERS = 8
HALF = 256
VMEM_LIMIT = 56 * 1024 * 1024


def place():
    section = lax.axis_index("section")
    rank = lax.axis_index("dp")
    y, z_hi = section // 2, section % 2
    x, z_lo, core = rank // 16, (rank % 16) // 2, rank % 2
    return x, y, z_hi, z_lo, core


def device(x, y, z_hi, z_lo, core):
    return (y * 2 + z_hi, x * 16 + z_lo * 2 + core)


def flip_low(v):
    return v + 1 - 2 * (v % 2)


def send(src, dst, send_sem, recv_sem, target):
    copy = pltpu.make_async_remote_copy(
        src_ref=src, dst_ref=dst, send_sem=send_sem, recv_sem=recv_sem,
        device_id=target, device_id_type=MESH,
    )
    copy.start()
    return copy


def meet(targets):
    barrier = pltpu.get_barrier_semaphore()
    for target in targets:
        pl.semaphore_signal(barrier, inc=1, device_id=target, device_id_type=MESH)
    pl.semaphore_wait(barrier, len(targets))


def gather_weights(w_ref, buf, mine_ref, sib_ref, sib_sem, z_send, z_recv, h_send, h_recv, c_send, c_recv):
    x, y, z_hi, z_lo, core = place()
    z = z_hi * 8 + z_lo
    sibling = device(x, y, z_hi, z_lo, 1 - core)
    z_peers = []
    for k in range(1, 16):
        other = (z + k) % 16
        z_peers.append(device(x, y, other // 8, other % 8, core))
    moves = [
        (lambda a, b: (flip_low(a), b)),
        (lambda a, b: (3 - a, b)),
        (lambda a, b: (a, flip_low(b))),
        (lambda a, b: (a, 3 - b)),
    ]
    orders = [(0, 1, 2, 3), (1, 2, 3, 0), (2, 3, 0, 1), (3, 0, 1, 2)]
    partners = []
    for move in moves:
        px, py = move(x, y)
        partners.append(device(px, py, z_hi, z_lo, core))
    meet([sibling] + z_peers + partners)

    first = core == 0
    wf = w_ref[...].astype(jnp.float32)
    left, right = wf[:, :256], wf[:, 256:]
    mine_ref[...] = jnp.where(first, right, left)
    swap = send(mine_ref, sib_ref, sib_sem.at[0], sib_sem.at[1], sibling)
    mine = jnp.where(first, left, right)
    swap.wait()
    theirs = sib_ref[...]
    rows = jnp.concatenate([jnp.where(first, mine, theirs), jnp.where(first, theirs, mine)], axis=0)
    own = buf.at[core, y, z_hi, x, pl.ds(pl.multiple_of(z_lo * 16, 16), 16), :]
    own[...] = rows.astype(jnp.bfloat16)
    z_copies = [send(own, own, z_send.at[k], z_recv.at[k], z_peers[k - 1]) for k in range(1, 16)]
    for copy in z_copies:
        copy.wait_recv()

    def block(j, at):
        bx, by = at
        return buf.at[core, by, j // 2, bx, pl.ds((j % 2) * 64, 64), :]

    held = {}
    copies = {}
    across = {}

    def forward(j, r, step_from):
        ref = block(j, held[j, r])
        for step in range(step_from, 4):
            index = 2 ** step + r
            copies[j, index] = send(
                ref, ref, h_send.at[j, index], h_recv.at[j, index], partners[orders[j][step]]
            )
        across[j, r] = send(ref, ref, c_send.at[j, r], c_recv.at[j, r], sibling)

    for j in range(4):
        held[j, 0] = (x, y)
        for r in range(1, 16):
            step = r.bit_length() - 1
            held[j, r] = moves[orders[j][step]](*held[j, r - 2 ** step])
    for j in range(4):
        forward(j, 0, 0)
    arrivals = sorted(range(1, 16), key=lambda r: (bin(r).count("1"), r))
    for r in arrivals:
        for j in range(4):
            copies[j, r].wait_recv()
            forward(j, r, r.bit_length())
    for j in range(4):
        for r in range(16):
            across[j, r].wait_recv()
    for copy in z_copies:
        copy.wait_send()
    for j in range(4):
        for r in range(16):
            across[j, r].wait_send()
            if r:
                copies[j, r].wait_send()


def gelu_parts(h):
    coeff = 0.7978845608028654
    inner = coeff * (h + 0.044715 * h * h * h)
    tanh_val = jnp.tanh(inner)
    value = 0.5 * h * (1.0 + tanh_val)
    slope = 0.5 * (1.0 + tanh_val) + 0.5 * h * (1.0 - tanh_val * tanh_val) * coeff * (
        1.0 + 3.0 * 0.044715 * h * h
    )
    return (value, slope)


def dot(a, b, dims):
    return lax.dot_general(
        a, b, ((dims[:1], dims[1:]), ((), ())), preferred_element_type=jnp.float32
    )


def splat(value):
    return jnp.broadcast_to(value, (8, 128))


def thirds(value):
    high = value.astype(jnp.bfloat16).astype(jnp.float32)
    rest = value - high
    middle = rest.astype(jnp.bfloat16).astype(jnp.float32)
    return high, middle, rest - middle


def product(a, b, dims, axes):
    a0, a1, a2 = thirds(a)
    b0, b1, b2 = thirds(b)
    long_a = jnp.concatenate([a0, a0, a1, a1, a0, a2], axis=axes[0]).astype(jnp.bfloat16)
    long_b = jnp.concatenate([b0, b1, b0, b1, b2, b0], axis=axes[1]).astype(jnp.bfloat16)
    return dot(long_a, long_b, dims)


def minus_inverse(e):
    at = lambda i, k: (min(i, k), max(i, k))
    for k in range(0, 8, 2):
        a, b, c = e[k, k], e[k, k + 1], e[k + 1, k + 1]
        scale = 1.0 / (a * c - b * b)
        ia, ib, ic = c * scale, -(b * scale), a * scale
        others = [i for i in range(8) if i not in (k, k + 1)]
        r0 = {i: ia * e[at(i, k)] + ib * e[at(i, k + 1)] for i in others}
        r1 = {i: ib * e[at(i, k)] + ic * e[at(i, k + 1)] for i in others}
        for i in others:
            for j in others:
                if i <= j:
                    e[i, j] = e[i, j] - (e[at(i, k)] * r0[j] + e[at(i, k + 1)] * r1[j])
        for i in others:
            e[at(i, k)], e[at(i, k + 1)] = r0[i], r1[i]
        e[k, k], e[k, k + 1], e[k + 1, k + 1] = -ia, -ib, -ic
    return lambda i, k: e[at(i, k)]


def sweep_pair(tiles):
    tiles = list(tiles)
    lane = lax.broadcasted_iota(jnp.int32, (8, 128), 1)
    row = lax.broadcasted_iota(jnp.int32, (8, 128), 0)
    first = lane < 64
    local_lane = lane % 64

    def column(tile, k):
        return jnp.where(first, splat(tile[:, k:k + 1]), splat(tile[:, 64 + k:65 + k]))

    for p in range(8):
        pivot = tiles[p]
        base = 8 * p
        in_block = (local_lane >= base) & (local_lane < base + 8)
        columns = [column(pivot, base + k) for k in range(8)]
        e = {}
        for k in range(8):
            for i in range(k + 1):
                e[i, k] = splat(columns[k][i:i + 1, :])
        inverse = minus_inverse(e)
        top = jnp.where(in_block, jnp.where(local_lane - base == row, 1.0, 0.0), -pivot)
        result = None
        for k in range(8):
            spread = inverse(0, k)
            for i in range(1, 8):
                spread = jnp.where(row == i, inverse(i, k), spread)
            term = spread * splat(top[k:k + 1, :])
            result = term if result is None else result + term
        tiles[p] = result
        if p < 7:
            value = jnp.where(in_block, 0.0, tiles[p + 1])
            for k in range(8):
                value = value - column(tiles[p + 1], base + k) * splat(result[k:k + 1, :])
        update = product(pivot, result, (0, 0), (0, 0))
        for i in range(8):
            if i not in (p, p + 1):
                step = jnp.where(first, update[8 * i:8 * i + 8], update[64 + 8 * i:72 + 8 * i])
                tiles[i] = jnp.where(in_block, 0.0, tiles[i]) - step
        if p < 7:
            tiles[p + 1] = value
    return tiles


def run_ahead(w_buf, xs, slopes, scales, u_own):
    section = lax.axis_index("section")

    def ahead(layer, carry):
        xf = xs[layer].astype(jnp.float32)
        scale = lax.rsqrt(jnp.mean(xf * xf, axis=-1, keepdims=True) + 1e-05)
        scales[layer] = jnp.broadcast_to(scale, (TOKENS, 128))
        unit = (xf * scale).astype(jnp.bfloat16)

        @pl.when(layer == section)
        def _():
            u_own[...] = unit

        for half in range(2):
            columns = slice(half * HALF, half * HALF + HALF)
            w_half = w_buf[half, layer // 2, layer % 2].reshape(WIDTH, HALF)
            value, slope = gelu_parts(dot(unit, w_half, (1, 0)))
            slopes[layer, :, columns] = slope
            xs[layer + 1, :, columns] = (xf[:, columns] + value).astype(jnp.bfloat16)
        return carry

    lax.fori_loop(0, LAYERS, ahead, 0)


def run_back(w_buf, xs, slopes, scales, grads, dh_own, beside):
    section = lax.axis_index("section")

    def back(step, carry):
        beside(step)
        layer = LAYERS - 1 - step
        grad = grads[...].astype(jnp.float32)
        d_h = (grad * slopes[layer]).astype(jnp.bfloat16)

        @pl.when(layer == section)
        def _():
            dh_own[...] = d_h

        d_u = None
        for half in range(2):
            w_half = w_buf[half, layer // 2, layer % 2].reshape(WIDTH, HALF)
            term = dot(d_h[:, half * HALF:half * HALF + HALF], w_half, (1, 1))
            d_u = term if d_u is None else d_u + term
        xf = xs[layer].astype(jnp.float32)
        scale = scales[layer, :, 0:1]
        shift = scale * scale * scale * jnp.mean(d_u * xf, axis=-1, keepdims=True)
        grads[...] = (grad + (scale * d_u - xf * shift)).astype(jnp.bfloat16)
        return carry

    lax.fori_loop(0, LAYERS, back, 0)


def keep(ref, at, value):
    for i in range(value.shape[1] // 128):
        ref[at + i * HALF:at + i * HALF + HALF, :] = value[:, i * 128:i * 128 + 128]


class Stream:
    def __init__(self, index, refs, sems, swap_x):
        self.part, self.acc, self.full, *self.got = refs
        self.sems, self.index = sems, index
        self.rows = self.part.shape[0]
        x, y, z_hi, z_lo, core = place()
        self.core = core
        self.sibling = device(x, y, z_hi, z_lo, 1 - core)
        steps = [
            (((x + 1) // 2) % 2, device(flip_low(x), y, z_hi, z_lo, core)),
            (x // 2, device(3 - x, y, z_hi, z_lo, core)),
        ]
        if swap_x:
            steps.reverse()
        for bit, distance in ((z_lo % 2, 1), ((z_lo // 2) % 2, 2), (z_lo // 4, 4)):
            steps.append((bit, device(x, y, z_hi, z_lo + distance * (1 - 2 * bit), core)))
        base = 0
        self.sent, self.kept, self.peers = [0], [0], [self.sibling]
        for t, (bit, peer) in enumerate(steps, 1):
            size = self.rows // 2 >> t
            self.sent.append(base + (1 - bit) * size)
            base = base + bit * size
            self.kept.append(base)
            self.peers.append(peer)

    def span(self, at, size):
        return pl.ds(pl.multiple_of(at, 8), size)

    def copy(self, t):
        half = self.rows // 2
        if t == 0:
            src, dst, peer = self.part.at[self.span((1 - self.core) * half, half)], self.got[0], self.sibling
        elif t <= 5:
            size = half >> t
            src, dst, peer = self.acc.at[self.span(self.sent[t], size)], self.got[t], self.peers[t]
        else:
            k = 11 - t
            src = self.full.at[self.span(self.core * half + self.kept[k], half >> k)]
            dst, peer = src, self.peers[k]
        return pltpu.make_async_remote_copy(
            src_ref=src, dst_ref=dst, send_sem=self.sems.at[0, self.index, t],
            recv_sem=self.sems.at[1, self.index, t], device_id=peer, device_id_type=MESH,
        )

    def advance(self, t):
        half = self.rows // 2
        if t > 0:
            done = t - 1
            self.copy(done).wait_recv()
            if done == 0:
                self.acc[...] = self.part[self.span(self.core * half, half), :] + self.got[0][...]
            elif done <= 5:
                mine = self.span(self.kept[done], half >> done)
                total = self.acc[mine, :] + self.got[done][...]
                if done < 5:
                    self.acc[mine, :] = total
                else:
                    self.full[self.span(self.core * half + self.kept[5], half >> 5), :] = total
        if t < 12:
            self.copy(t).start()

    def close(self):
        for t in range(12):
            self.copy(t).wait_send()


def load_factor(mats, which, small, large):
    row = lax.broadcasted_iota(jnp.int32, (128, 128), 0)
    lane = lax.broadcasted_iota(jnp.int32, (128, 128), 1)
    shift = jnp.where(row == lane, 0.1, 0.0)
    share = 1.0 / 32768.0

    def put(i, j, value):
        value = value * share
        mats[which, i * 128:i * 128 + 128, j * 128:j * 128 + 128] = value + shift if i == j else value

    for i in range(2):
        for j in range(2):
            low = large[j * HALF + i * 128:j * HALF + i * 128 + 128, :]
            put(i, j, small[j * HALF + i * 128:j * HALF + i * 128 + 128, :])
            put(2 + i, j, low)
            put(j, 2 + i, low.T)
            put(2 + i, 2 + j, large[WIDTH + j * HALF + i * 128:WIDTH + j * HALF + i * 128 + 128, :])


def invert(mats, beside):
    wide_lane = lax.broadcasted_iota(jnp.int32, (64, WIDTH), 1)
    wide_row = lax.broadcasted_iota(jnp.int32, (64, WIDTH), 0)

    def eliminate(block, carry):
        for odd in range(2):
            for b in range(4):
                pl.when(block == b)(functools.partial(beside, 2 * b + odd))
            at = pl.multiple_of(block * 128 + odd * 64, 64)
            rows = pl.ds(at, 64)
            pair = []
            for which in range(2):
                square = mats[which, rows, pl.ds(pl.multiple_of(block * 128, 128), 128)]
                pair.append(square[:, odd * 64:odd * 64 + 64])
            both = jnp.concatenate(pair, axis=1)
            done = jnp.concatenate(sweep_pair([both[8 * i:8 * i + 8] for i in range(8)]), axis=0)
            in_block = (wide_lane >= at) & (wide_lane < at + 64)
            for which in range(2):
                panel = mats[which, rows, :]
                top = jnp.where(in_block, jnp.where(wide_lane - at == wide_row, 1.0, 0.0), -panel)
                fresh = product(done[:, which * 64:which * 64 + 64], top, (1, 0), (1, 0))
                for part in range(2):
                    half = pl.ds(part * 256, 256)
                    step = product(panel[:, part * 256:part * 256 + 256], fresh, (0, 0), (0, 0))
                    mats[which, half, :] = jnp.where(in_block[:1], 0.0, mats[which, half, :]) - step
                mats[which, rows, :] = fresh
        return carry

    lax.fori_loop(0, 4, eliminate, 0)


def packed(ref):
    return jnp.concatenate([ref[i * HALF:i * HALF + HALF, :] for i in range(4)], axis=1)


def kernel(act_ref, cot_ref, w_ref, out_ref, w_buf, xs, slopes, scales, grads, u_own, dh_own, mats, p_mat, *rest):
    gather_refs, sems, stream_refs = rest[:9], rest[9], rest[10:]
    rank = lax.axis_index("dp")
    streams = []
    for i in range(6):
        streams.append(Stream(i, stream_refs[9 * i:9 * i + 9], sems, i % 2 == 1))
    a_small, a_large, g_small, g_large, d_top, d_low = streams

    xs[0] = act_ref[...]
    grads[...] = cot_ref[...]
    gather_weights(w_ref, w_buf, *gather_refs)
    run_ahead(w_buf, xs, slopes, scales, u_own)

    def factor(ref, small, large):
        keep(small.part, 0, dot(ref[:, :HALF], ref[:, :HALF], (0, 0)))
        keep(large.part, 0, dot(ref[:, HALF:], ref[:, :HALF], (0, 0)))
        keep(large.part, WIDTH, dot(ref[:, HALF:], ref[:, HALF:], (0, 0)))

    def advance(group, t):
        for stream in group:
            stream.advance(t)

    in_pair, out_pair, d_pair = streams[:2], streams[2:4], streams[4:]
    factor(u_own, a_small, a_large)
    advance(in_pair, 0)

    def beside_back(step):
        for t in range(1, 5):
            pl.when(step == 2 * t - 1)(functools.partial(advance, in_pair, t))

    run_back(w_buf, xs, slopes, scales, grads, dh_own, beside_back)
    factor(dh_own, g_small, g_large)
    advance(out_pair, 0)
    keep(d_top.part, 0, dot(u_own[:, :HALF], dh_own[...], (0, 0)))
    keep(d_low.part, 0, dot(u_own[:, HALF:], dh_own[...], (0, 0)))
    for t in range(1, 13):
        advance(out_pair, t)
        if t + 4 <= 12:
            advance(in_pair, t + 4)
        if t + 4 == 12:
            load_factor(mats, 0, a_small.full, a_large.full)
        if t >= 8:
            advance(d_pair, t - 8)
    load_factor(mats, 1, g_small.full, g_large.full)

    def beside_invert(step):
        advance(d_pair, 5 + step)

    invert(mats, beside_invert)
    d_mat = jnp.concatenate([packed(d_top.full), packed(d_low.full)], axis=0)
    p_mat[...] = product(mats[0], d_mat, (1, 0), (1, 0))
    p_mat[...] = product(p_mat[...], mats[1], (1, 0), (1, 0))
    whole = p_mat[...]
    mean = jnp.sum(jnp.sum(whole * whole, axis=0, keepdims=True), axis=1, keepdims=True) * (1.0 / (WIDTH * WIDTH))
    mine = p_mat[pl.ds(pl.multiple_of(rank * 8, 8), 8), :]
    out_ref[...] = mine / jnp.sqrt(mean + 1e-06)
    for stream in streams:
        stream.close()


def local(first_acts, cotangent, weights):
    square = lambda n, kind: pltpu.VMEM((n, TOKENS, WIDTH), kind)
    flat = lambda kind: pltpu.VMEM((TOKENS, WIDTH), kind)
    copies = pltpu.SemaphoreType.DMA
    scratch = [
        pltpu.VMEM((2, 4, 2, 4, 128, HALF), jnp.bfloat16),
        square(LAYERS + 1, jnp.bfloat16),
        square(LAYERS, jnp.float32),
        pltpu.VMEM((LAYERS, TOKENS, 128), jnp.float32),
        flat(jnp.bfloat16), flat(jnp.bfloat16), flat(jnp.bfloat16),
        square(2, jnp.float32), flat(jnp.float32),
        pltpu.VMEM((8, HALF), jnp.float32),
        pltpu.VMEM((8, HALF), jnp.float32),
        copies((2,)), copies((16,)), copies((16,)),
        copies((4, 16)), copies((4, 16)), copies((4, 16)), copies((4, 16)),
        copies((2, 6, 12)),
    ]
    for rows in (512, 1024, 512, 1024, 1024, 1024):
        sizes = [rows, rows // 2, rows] + [rows // 2 >> t for t in range(6)]
        scratch += [pltpu.VMEM((size, 128), jnp.float32) for size in sizes]
    return pl.pallas_call(
        kernel,
        out_shape=jax.ShapeDtypeStruct((8, WIDTH), jnp.float32),
        in_specs=[pl.BlockSpec(memory_space=pltpu.VMEM)] * 3,
        out_specs=pl.BlockSpec(memory_space=pltpu.VMEM),
        scratch_shapes=scratch,
        compiler_params=pltpu.CompilerParams(
            collective_id=0, has_side_effects=True, vmem_limit_bytes=VMEM_LIMIT
        ),
        name="chain_and_factors",
    )(first_acts.reshape(TOKENS, WIDTH), cotangent.reshape(TOKENS, WIDTH), weights)


def solution(mesh):
    placed = (P(None, "dp", None), P(None, "dp", None), P(("section", "dp"), None))
    return jax.shard_map(
        local, mesh=mesh, in_specs=placed, out_specs=P(("section", "dp"), None), check_vma=False
    )
```

time: 1780 us -> 159 us (0.09)
  the two profiles are of different devices: /device:TPU:1 before, /device:TPU:8 now
where the time goes in v2:
time: 159 us; the launch traced here: 158 us
  Pallas kernels  157 us (99%)
    pallas_call x1, Pallas kernels, local(): pl.pallas_call(kernel, out_shape=jax.ShapeDtypeStruct((8, WIDTH), jnp.flo...  157 us

profile of v2, /device:TPU:8, one launch (start us, length us, event | category | flops | bytes accessed | tf_op | source)
XLA Modules:
  0.0 158.3 jit_solution(13592642222528560710)
XLA Ops:
  0.0 157.0 %chain_and_factors.1 = f32[8,512]{1,0:T(8,128)} custom-call(bf16[512,512]{1,0:T(8,128)(2,1)} %bitcast.2, bf16[512,512]{1,0:T(8,128)(2,1)} %bitcast.3, bf16[8,512]{1,0:T(8,128)(2,1)} %w_ref.1), custom_call_target="tpu_custom_call" | custom-call | tf_op jit(solution)/shard_map/chain_and_factors/pallas_call | solution.py:481
  157.0 1.3 copy.5

commit v3 on v2

--- a/solution.py
+++ b/solution.py
@@ -270,7 +270,11 @@
         grads[...] = (grad + (scale * d_u - xf * shift)).astype(jnp.bfloat16)
         return carry
 
-    lax.fori_loop(0, LAYERS, back, 0)
+    lax.fori_loop(0, LAYERS - 1, back, 0)
+
+    @pl.when(section == 0)
+    def _():
+        dh_own[...] = (grads[...].astype(jnp.float32) * slopes[0]).astype(jnp.bfloat16)
 
 
 def keep(ref, at, value):
@@ -279,12 +283,15 @@
 
 
 class Stream:
-    def __init__(self, index, refs, sems, swap_x):
-        self.part, self.acc, self.full, *self.got = refs
-        self.sems, self.index = sems, index
-        self.rows = self.part.shape[0]
+    LAST = 8
+
+    def __init__(self, index, refs, sems, z_sems, swap_x):
+        self.part, self.acc, self.full, self.got_core, self.got_one, self.got_two, self.got_z = refs
+        self.sems, self.z_sems, self.index = sems, z_sems, index
+        self.half = self.part.shape[0] // 2
+        self.chunk = self.half // 32
         x, y, z_hi, z_lo, core = place()
-        self.core = core
+        self.core, self.z_lo = core, z_lo
         self.sibling = device(x, y, z_hi, z_lo, 1 - core)
         steps = [
             (((x + 1) // 2) % 2, device(flip_low(x), y, z_hi, z_lo, core)),
@@ -292,29 +299,28 @@
         ]
         if swap_x:
             steps.reverse()
-        for bit, distance in ((z_lo % 2, 1), ((z_lo // 2) % 2, 2), (z_lo // 4, 4)):
-            steps.append((bit, device(x, y, z_hi, z_lo + distance * (1 - 2 * bit), core)))
         base = 0
         self.sent, self.kept, self.peers = [0], [0], [self.sibling]
         for t, (bit, peer) in enumerate(steps, 1):
-            size = self.rows // 2 >> t
+            size = self.half >> t
             self.sent.append(base + (1 - bit) * size)
             base = base + bit * size
             self.kept.append(base)
             self.peers.append(peer)
+        self.z_peers = [device(x, y, z_hi, (z_lo + k) % 8, core) for k in range(8)]
 
     def span(self, at, size):
         return pl.ds(pl.multiple_of(at, 8), size)
 
     def copy(self, t):
-        half = self.rows // 2
+        half = self.half
         if t == 0:
-            src, dst, peer = self.part.at[self.span((1 - self.core) * half, half)], self.got[0], self.sibling
-        elif t <= 5:
-            size = half >> t
-            src, dst, peer = self.acc.at[self.span(self.sent[t], size)], self.got[t], self.peers[t]
+            src, dst, peer = self.part.at[self.span((1 - self.core) * half, half)], self.got_core, self.sibling
+        elif t <= 2:
+            src, peer = self.acc.at[self.span(self.sent[t], half >> t)], self.peers[t]
+            dst = self.got_one if t == 1 else self.got_two
         else:
-            k = 11 - t
+            k = 7 - t
             src = self.full.at[self.span(self.core * half + self.kept[k], half >> k)]
             dst, peer = src, self.peers[k]
         return pltpu.make_async_remote_copy(
@@ -322,26 +328,54 @@
             recv_sem=self.sems.at[1, self.index, t], device_id=peer, device_id_type=MESH,
         )
 
+    def summed(self, z_lo):
+        return self.span(self.core * self.half + self.kept[2] + z_lo * self.chunk, self.chunk)
+
+    def z_copy(self, t, k, arriving=False):
+        if t == 3:
+            there = (self.z_lo + k) % 8
+            src = self.acc.at[self.span(self.kept[2] + there * self.chunk, self.chunk)]
+            dst = self.got_z.at[k - 1]
+        else:
+            src = self.full.at[self.summed((self.z_lo + 8 - k) % 8 if arriving else self.z_lo)]
+            dst = src
+        return pltpu.make_async_remote_copy(
+            src_ref=src, dst_ref=dst, send_sem=self.z_sems.at[0, t - 3, self.index, k],
+            recv_sem=self.z_sems.at[1, t - 3, self.index, k], device_id=self.z_peers[k], device_id_type=MESH,
+        )
+
     def advance(self, t):
-        half = self.rows // 2
         if t > 0:
             done = t - 1
-            self.copy(done).wait_recv()
+            if done in (3, 4):
+                for k in range(1, 8):
+                    self.z_copy(done, k, True).wait_recv()
+            else:
+                self.copy(done).wait_recv()
             if done == 0:
-                self.acc[...] = self.part[self.span(self.core * half, half), :] + self.got[0][...]
-            elif done <= 5:
-                mine = self.span(self.kept[done], half >> done)
-                total = self.acc[mine, :] + self.got[done][...]
-                if done < 5:
-                    self.acc[mine, :] = total
-                else:
-                    self.full[self.span(self.core * half + self.kept[5], half >> 5), :] = total
-        if t < 12:
+                self.acc[...] = self.part[self.span(self.core * self.half, self.half), :] + self.got_core[...]
+            elif done <= 2:
+                mine = self.span(self.kept[done], self.half >> done)
+                got = self.got_one if done == 1 else self.got_two
+                self.acc[mine, :] = self.acc[mine, :] + got[...]
+            elif done == 3:
+                total = self.acc[self.span(self.kept[2] + self.z_lo * self.chunk, self.chunk), :]
+                for k in range(7):
+                    total = total + self.got_z[k]
+                self.full[self.summed(self.z_lo), :] = total
+        if t in (3, 4):
+            for k in (4, 3, 5, 2, 6, 1, 7):
+                self.z_copy(t, k).start()
+        elif t < 8:
             self.copy(t).start()
 
     def close(self):
-        for t in range(12):
-            self.copy(t).wait_send()
+        for t in range(8):
+            if t in (3, 4):
+                for k in range(1, 8):
+                    self.z_copy(t, k).wait_send()
+            else:
+                self.copy(t).wait_send()
 
 
 def load_factor(mats, which, small, large):
@@ -399,11 +433,11 @@
 
 
 def kernel(act_ref, cot_ref, w_ref, out_ref, w_buf, xs, slopes, scales, grads, u_own, dh_own, mats, p_mat, *rest):
-    gather_refs, sems, stream_refs = rest[:9], rest[9], rest[10:]
+    gather_refs, sems, z_sems, stream_refs = rest[:9], rest[9], rest[10], rest[11:]
     rank = lax.axis_index("dp")
     streams = []
     for i in range(6):
-        streams.append(Stream(i, stream_refs[9 * i:9 * i + 9], sems, i % 2 == 1))
+        streams.append(Stream(i, stream_refs[7 * i:7 * i + 7], sems, z_sems, i % 2 == 1))
     a_small, a_large, g_small, g_large, d_top, d_low = streams
 
     xs[0] = act_ref[...]
@@ -425,26 +459,27 @@
     advance(in_pair, 0)
 
     def beside_back(step):
-        for t in range(1, 5):
-            pl.when(step == 2 * t - 1)(functools.partial(advance, in_pair, t))
+        for t, at in ((1, 2), (2, 4), (3, 6)):
+            pl.when(step == at)(functools.partial(advance, in_pair, t))
 
     run_back(w_buf, xs, slopes, scales, grads, dh_own, beside_back)
     factor(dh_own, g_small, g_large)
     advance(out_pair, 0)
     keep(d_top.part, 0, dot(u_own[:, :HALF], dh_own[...], (0, 0)))
     keep(d_low.part, 0, dot(u_own[:, HALF:], dh_own[...], (0, 0)))
-    for t in range(1, 13):
+    for t in range(1, 9):
         advance(out_pair, t)
-        if t + 4 <= 12:
-            advance(in_pair, t + 4)
-        if t + 4 == 12:
+        if t + 3 <= 8:
+            advance(in_pair, t + 3)
+        if t + 3 == 8:
             load_factor(mats, 0, a_small.full, a_large.full)
-        if t >= 8:
-            advance(d_pair, t - 8)
+        if t >= 2:
+            advance(d_pair, t - 2)
     load_factor(mats, 1, g_small.full, g_large.full)
 
     def beside_invert(step):
-        advance(d_pair, 5 + step)
+        if step in (2, 4):
+            advance(d_pair, 6 + step // 2)
 
     invert(mats, beside_invert)
     d_mat = jnp.concatenate([packed(d_top.full), packed(d_low.full)], axis=0)
@@ -473,11 +508,12 @@
         pltpu.VMEM((8, HALF), jnp.float32),
         copies((2,)), copies((16,)), copies((16,)),
         copies((4, 16)), copies((4, 16)), copies((4, 16)), copies((4, 16)),
-        copies((2, 6, 12)),
+        copies((2, 6, 8)), copies((2, 2, 6, 8)),
     ]
     for rows in (512, 1024, 512, 1024, 1024, 1024):
-        sizes = [rows, rows // 2, rows] + [rows // 2 >> t for t in range(6)]
+        sizes = [rows, rows // 2, rows, rows // 2, rows // 4, rows // 8]
         scratch += [pltpu.VMEM((size, 128), jnp.float32) for size in sizes]
+        scratch.append(pltpu.VMEM((7, rows // 64, 128), jnp.float32))
     return pl.pallas_call(
         kernel,
         out_shape=jax.ShapeDtypeStruct((8, WIDTH), jnp.float32),

time: 159 us -> 148 us (0.931)
  Pallas kernels: 157 us -> 146 us
    pallas_call x1, Pallas kernels: 157 us -> 146 us  [local(): pl.pallas_call(kernel, out_shape=jax.ShapeDtypeStruct((8, WIDTH), jnp.flo...]
where the time goes in v3:
time: 148 us; the launch traced here: 147 us
  Pallas kernels  146 us (99%)
    pallas_call x1, Pallas kernels, local(): pl.pallas_call(kernel, out_shape=jax.ShapeDtypeStruct((8, WIDTH), jnp.flo...  146 us

profile of v3, /device:TPU:8, one launch (start us, length us, event | category | flops | bytes accessed | tf_op | source)
XLA Modules:
  0.0 147.3 jit_solution(10248086388689782446)
XLA Ops:
  0.0 146.0 %chain_and_factors.1 = f32[8,512]{1,0:T(8,128)} custom-call(bf16[512,512]{1,0:T(8,128)(2,1)} %bitcast.2, bf16[512,512]{1,0:T(8,128)(2,1)} %bitcast.3, bf16[8,512]{1,0:T(8,128)(2,1)} %w_ref.1), custom_call_target="tpu_custom_call" | custom-call | tf_op jit(solution)/shard_map/chain_and_factors/pallas_call | solution.py:517
  146.0 1.3 copy.5

commit v4 on v2

--- a/solution.py
+++ b/solution.py
@@ -66,7 +66,7 @@
     for move in moves:
         px, py = move(x, y)
         partners.append(device(px, py, z_hi, z_lo, core))
-    meet([sibling] + z_peers + partners)
+    meet([sibling] + z_peers + partners + [device((x + 2) % 4, y, z_hi, z_lo, core)])
 
     first = core == 0
     wf = w_ref[...].astype(jnp.float32)
@@ -158,6 +158,17 @@
     long_a = jnp.concatenate([a0, a0, a1, a1, a0, a2], axis=axes[0]).astype(jnp.bfloat16)
     long_b = jnp.concatenate([b0, b1, b0, b1, b2, b0], axis=axes[1]).astype(jnp.bfloat16)
     return dot(long_a, long_b, dims)
+
+
+def halves(value):
+    high = value.astype(jnp.bfloat16)
+    return high, (value - high.astype(jnp.float32)).astype(jnp.bfloat16)
+
+
+def product_of_halves(a, b):
+    a0, a1 = halves(a)
+    b0, b1 = halves(b)
+    return dot(a0, b0, (1, 0)) + (dot(a0, b1, (1, 0)) + dot(a1, b0, (1, 0)))
 
 
 def minus_inverse(e):
@@ -270,7 +281,11 @@
         grads[...] = (grad + (scale * d_u - xf * shift)).astype(jnp.bfloat16)
         return carry
 
-    lax.fori_loop(0, LAYERS, back, 0)
+    lax.fori_loop(0, LAYERS - 1, back, 0)
+
+    @pl.when(section == 0)
+    def _():
+        dh_own[...] = (grads[...].astype(jnp.float32) * slopes[0]).astype(jnp.bfloat16)
 
 
 def keep(ref, at, value):
@@ -279,69 +294,85 @@
 
 
 class Stream:
-    def __init__(self, index, refs, sems, swap_x):
-        self.part, self.acc, self.full, *self.got = refs
+    def __init__(self, index, refs, sems, x_sems, z_sems):
+        self.part, self.acc, self.full, self.got_core, self.got_x, self.got_z = refs
         self.sems, self.index = sems, index
-        self.rows = self.part.shape[0]
+        self.half = self.part.shape[0] // 2
         x, y, z_hi, z_lo, core = place()
         self.core = core
         self.sibling = device(x, y, z_hi, z_lo, 1 - core)
-        steps = [
-            (((x + 1) // 2) % 2, device(flip_low(x), y, z_hi, z_lo, core)),
-            (x // 2, device(3 - x, y, z_hi, z_lo, core)),
-        ]
-        if swap_x:
-            steps.reverse()
-        for bit, distance in ((z_lo % 2, 1), ((z_lo // 2) % 2, 2), (z_lo // 4, 4)):
-            steps.append((bit, device(x, y, z_hi, z_lo + distance * (1 - 2 * bit), core)))
-        base = 0
-        self.sent, self.kept, self.peers = [0], [0], [self.sibling]
-        for t, (bit, peer) in enumerate(steps, 1):
-            size = self.rows // 2 >> t
-            self.sent.append(base + (1 - bit) * size)
-            base = base + bit * size
-            self.kept.append(base)
-            self.peers.append(peer)
+        x_peers = [device((x + k) % 4, y, z_hi, z_lo, core) for k in range(4)]
+        z_peers = [device(x, y, z_hi, (z_lo + k) % 8, core) for k in range(8)]
+        third = x * (self.half // 4)
+        self.ways = {"x": (4, x, 0, x_peers, x_sems, self.got_x), "z": (8, z_lo, third, z_peers, z_sems, self.got_z)}
 
     def span(self, at, size):
         return pl.ds(pl.multiple_of(at, 8), size)
 
-    def copy(self, t):
-        half = self.rows // 2
+    def core_copy(self, t):
+        half = self.half
         if t == 0:
-            src, dst, peer = self.part.at[self.span((1 - self.core) * half, half)], self.got[0], self.sibling
-        elif t <= 5:
-            size = half >> t
-            src, dst, peer = self.acc.at[self.span(self.sent[t], size)], self.got[t], self.peers[t]
+            src, dst = self.part.at[self.span((1 - self.core) * half, half)], self.got_core
         else:
-            k = 11 - t
-            src = self.full.at[self.span(self.core * half + self.kept[k], half >> k)]
-            dst, peer = src, self.peers[k]
+            src = self.full.at[self.span(self.core * half, half)]
+            dst = src
         return pltpu.make_async_remote_copy(
-            src_ref=src, dst_ref=dst, send_sem=self.sems.at[0, self.index, t],
-            recv_sem=self.sems.at[1, self.index, t], device_id=peer, device_id_type=MESH,
+            src_ref=src, dst_ref=dst, send_sem=self.sems.at[0, self.index, t // 5],
+            recv_sem=self.sems.at[1, self.index, t // 5], device_id=self.sibling, device_id_type=MESH,
         )
 
+    def copies(self, t, arriving=False):
+        count, mine, base, peers, sems, got = self.ways["x" if t in (1, 4) else "z"]
+        size = got.shape[1]
+        way = 0 if t <= 2 else 1
+        made = []
+        for k in range(1, count):
+            if way == 0:
+                src, dst = self.acc.at[self.span(base + (mine + k) % count * size, size)], got.at[k - 1]
+            else:
+                owner = (mine + count - k) % count if arriving else mine
+                src = self.full.at[self.span(self.core * self.half + base + owner * size, size)]
+                dst = src
+            made.append(pltpu.make_async_remote_copy(
+                src_ref=src, dst_ref=dst, send_sem=sems.at[0, way, self.index, k],
+                recv_sem=sems.at[1, way, self.index, k], device_id=peers[k], device_id_type=MESH,
+            ))
+        return made
+
     def advance(self, t):
-        half = self.rows // 2
         if t > 0:
             done = t - 1
-            self.copy(done).wait_recv()
+            if done in (0, 5):
+                self.core_copy(done).wait_recv()
+            else:
+                for copy in self.copies(done, True):
+                    copy.wait_recv()
             if done == 0:
-                self.acc[...] = self.part[self.span(self.core * half, half), :] + self.got[0][...]
-            elif done <= 5:
-                mine = self.span(self.kept[done], half >> done)
-                total = self.acc[mine, :] + self.got[done][...]
-                if done < 5:
-                    self.acc[mine, :] = total
+                self.acc[...] = self.part[self.span(self.core * self.half, self.half), :] + self.got_core[...]
+            elif done <= 2:
+                count, mine, base, _, _, got = self.ways["x" if done == 1 else "z"]
+                size = got.shape[1]
+                here = self.span(base + mine * size, size)
+                total = self.acc[here, :]
+                for k in range(count - 1):
+                    total = total + got[k]
+                if done == 1:
+                    self.acc[here, :] = total
                 else:
-                    self.full[self.span(self.core * half + self.kept[5], half >> 5), :] = total
-        if t < 12:
-            self.copy(t).start()
+                    self.full[self.span(self.core * self.half + base + mine * size, size), :] = total
+        if t in (0, 5):
+            self.core_copy(t).start()
+        elif t < 5:
+            for copy in self.copies(t):
+                copy.start()
 
     def close(self):
-        for t in range(12):
-            self.copy(t).wait_send()
+        for t in range(6):
+            if t in (0, 5):
+                self.core_copy(t).wait_send()
+            else:
+                for copy in self.copies(t):
+                    copy.wait_send()
 
 
 def load_factor(mats, which, small, large):
@@ -399,11 +430,11 @@
 
 
 def kernel(act_ref, cot_ref, w_ref, out_ref, w_buf, xs, slopes, scales, grads, u_own, dh_own, mats, p_mat, *rest):
-    gather_refs, sems, stream_refs = rest[:9], rest[9], rest[10:]
+    gather_refs, sems, x_sems, z_sems, stream_refs = rest[:9], rest[9], rest[10], rest[11], rest[12:]
     rank = lax.axis_index("dp")
     streams = []
     for i in range(6):
-        streams.append(Stream(i, stream_refs[9 * i:9 * i + 9], sems, i % 2 == 1))
+        streams.append(Stream(i, stream_refs[6 * i:6 * i + 6], sems, x_sems, z_sems))
     a_small, a_large, g_small, g_large, d_top, d_low = streams
 
     xs[0] = act_ref[...]
@@ -425,31 +456,32 @@
     advance(in_pair, 0)
 
     def beside_back(step):
-        for t in range(1, 5):
-            pl.when(step == 2 * t - 1)(functools.partial(advance, in_pair, t))
+        for t, at in ((1, 2), (2, 5)):
+            pl.when(step == at)(functools.partial(advance, in_pair, t))
 
     run_back(w_buf, xs, slopes, scales, grads, dh_own, beside_back)
     factor(dh_own, g_small, g_large)
     advance(out_pair, 0)
     keep(d_top.part, 0, dot(u_own[:, :HALF], dh_own[...], (0, 0)))
     keep(d_low.part, 0, dot(u_own[:, HALF:], dh_own[...], (0, 0)))
-    for t in range(1, 13):
+    for t in range(1, 7):
         advance(out_pair, t)
-        if t + 4 <= 12:
-            advance(in_pair, t + 4)
-        if t + 4 == 12:
+        if t + 2 <= 6:
+            advance(in_pair, t + 2)
+        if t + 2 == 6:
             load_factor(mats, 0, a_small.full, a_large.full)
-        if t >= 8:
-            advance(d_pair, t - 8)
+        if t >= 2:
+            advance(d_pair, t - 2)
     load_factor(mats, 1, g_small.full, g_large.full)
 
     def beside_invert(step):
-        advance(d_pair, 5 + step)
+        if step in (2, 4):
+            advance(d_pair, 4 + step // 2)
 
     invert(mats, beside_invert)
     d_mat = jnp.concatenate([packed(d_top.full), packed(d_low.full)], axis=0)
-    p_mat[...] = product(mats[0], d_mat, (1, 0), (1, 0))
-    p_mat[...] = product(p_mat[...], mats[1], (1, 0), (1, 0))
+    p_mat[...] = product_of_halves(mats[0], d_mat)
+    p_mat[...] = product_of_halves(p_mat[...], mats[1])
     whole = p_mat[...]
     mean = jnp.sum(jnp.sum(whole * whole, axis=0, keepdims=True), axis=1, keepdims=True) * (1.0 / (WIDTH * WIDTH))
     mine = p_mat[pl.ds(pl.multiple_of(rank * 8, 8), 8), :]
@@ -473,11 +505,12 @@
         pltpu.VMEM((8, HALF), jnp.float32),
         copies((2,)), copies((16,)), copies((16,)),
         copies((4, 16)), copies((4, 16)), copies((4, 16)), copies((4, 16)),
-        copies((2, 6, 12)),
+        copies((2, 6, 2)), copies((2, 2, 6, 4)), copies((2, 2, 6, 8)),
     ]
     for rows in (512, 1024, 512, 1024, 1024, 1024):
-        sizes = [rows, rows // 2, rows] + [rows // 2 >> t for t in range(6)]
+        sizes = [rows, rows // 2, rows, rows // 2]
         scratch += [pltpu.VMEM((size, 128), jnp.float32) for size in sizes]
+        scratch += [pltpu.VMEM((n - 1, rows // (2 * part), 128), jnp.float32) for n, part in ((4, 4), (8, 32))]
     return pl.pallas_call(
         kernel,
         out_shape=jax.ShapeDtypeStruct((8, WIDTH), jnp.float32),

time: 159 us -> 141 us (0.89)
  Pallas kernels: 157 us -> 140 us
    pallas_call x1, Pallas kernels: 157 us -> 140 us  [local(): pl.pallas_call(kernel, out_shape=jax.ShapeDtypeStruct((8, WIDTH), jnp.flo...]
where the time goes in v4:
time: 141 us
  Pallas kernels  140 us (99%)
    pallas_call x1, Pallas kernels, local(): pl.pallas_call(kernel, out_shape=jax.ShapeDtypeStruct((8, WIDTH), jnp.flo...  140 us

profile of v4, /device:TPU:8, one launch (start us, length us, event | category | flops | bytes accessed | tf_op | source)
XLA Modules:
  0.0 141.0 jit_solution(2418223511431886707)
XLA Ops:
  0.0 139.7 %chain_and_factors.1 = f32[8,512]{1,0:T(8,128)} custom-call(bf16[512,512]{1,0:T(8,128)(2,1)} %bitcast.2, bf16[512,512]{1,0:T(8,128)(2,1)} %bitcast.3, bf16[8,512]{1,0:T(8,128)(2,1)} %w_ref.1), custom_call_target="tpu_custom_call" | custom-call | tf_op jit(solution)/shard_map/chain_and_factors/pallas_call | solution.py:514
  139.7 1.3 copy.5

commit v5 on v4

--- a/solution.py
+++ b/solution.py
@@ -233,19 +233,14 @@
     return tiles
 
 
-def run_ahead(w_buf, xs, slopes, scales, u_own):
-    section = lax.axis_index("section")
-
+def run_ahead(w_buf, xs, slopes, scales, units):
     def ahead(layer, carry):
         xf = xs[layer].astype(jnp.float32)
         scale = lax.rsqrt(jnp.mean(xf * xf, axis=-1, keepdims=True) + 1e-05)
         scales[layer] = jnp.broadcast_to(scale, (TOKENS, 128))
         unit = (xf * scale).astype(jnp.bfloat16)
 
-        @pl.when(layer == section)
-        def _():
-            u_own[...] = unit
-
+        units[layer] = unit
         for half in range(2):
             columns = slice(half * HALF, half * HALF + HALF)
             w_half = w_buf[half, layer // 2, layer % 2].reshape(WIDTH, HALF)
@@ -257,19 +252,14 @@
     lax.fori_loop(0, LAYERS, ahead, 0)
 
 
-def run_back(w_buf, xs, slopes, scales, grads, dh_own, beside):
-    section = lax.axis_index("section")
-
+def run_back(w_buf, xs, slopes, scales, grads, slants, beside):
     def back(step, carry):
         beside(step)
         layer = LAYERS - 1 - step
         grad = grads[...].astype(jnp.float32)
         d_h = (grad * slopes[layer]).astype(jnp.bfloat16)
 
-        @pl.when(layer == section)
-        def _():
-            dh_own[...] = d_h
-
+        slants[layer] = d_h
         d_u = None
         for half in range(2):
             w_half = w_buf[half, layer // 2, layer % 2].reshape(WIDTH, HALF)
@@ -282,10 +272,7 @@
         return carry
 
     lax.fori_loop(0, LAYERS - 1, back, 0)
-
-    @pl.when(section == 0)
-    def _():
-        dh_own[...] = (grads[...].astype(jnp.float32) * slopes[0]).astype(jnp.bfloat16)
+    slants[0] = (grads[...].astype(jnp.float32) * slopes[0]).astype(jnp.bfloat16)
 
 
 def keep(ref, at, value):
@@ -415,9 +402,19 @@
                 panel = mats[which, rows, :]
                 top = jnp.where(in_block, jnp.where(wide_lane - at == wide_row, 1.0, 0.0), -panel)
                 fresh = product(done[:, which * 64:which * 64 + 64], top, (1, 0), (1, 0))
+                if which == 0:
+                    p0, p1 = halves(panel)
+                    f0, f1 = halves(fresh)
+                    wide, long = [p0, p0, p1], [f0, f1, f0]
+                else:
+                    p0, p1, p2 = thirds(panel)
+                    f0, f1, f2 = thirds(fresh)
+                    wide, long = [p0, p0, p1, p1, p0, p2], [f0, f1, f0, f1, f2, f0]
+                wide = jnp.concatenate(wide, axis=0).astype(jnp.bfloat16)
+                long = jnp.concatenate(long, axis=0).astype(jnp.bfloat16)
                 for part in range(2):
                     half = pl.ds(part * 256, 256)
-                    step = product(panel[:, part * 256:part * 256 + 256], fresh, (0, 0), (0, 0))
+                    step = dot(wide[:, part * 256:part * 256 + 256], long, (0, 0))
                     mats[which, half, :] = jnp.where(in_block[:1], 0.0, mats[which, half, :]) - step
                 mats[which, rows, :] = fresh
         return carry
@@ -429,9 +426,9 @@
     return jnp.concatenate([ref[i * HALF:i * HALF + HALF, :] for i in range(4)], axis=1)
 
 
-def kernel(act_ref, cot_ref, w_ref, out_ref, w_buf, xs, slopes, scales, grads, u_own, dh_own, mats, p_mat, *rest):
+def kernel(act_ref, cot_ref, w_ref, out_ref, w_buf, xs, slopes, scales, grads, units, slants, mats, p_mat, *rest):
     gather_refs, sems, x_sems, z_sems, stream_refs = rest[:9], rest[9], rest[10], rest[11], rest[12:]
-    rank = lax.axis_index("dp")
+    section, rank = lax.axis_index("section"), lax.axis_index("dp")
     streams = []
     for i in range(6):
         streams.append(Stream(i, stream_refs[6 * i:6 * i + 6], sems, x_sems, z_sems))
@@ -440,7 +437,8 @@
     xs[0] = act_ref[...]
     grads[...] = cot_ref[...]
     gather_weights(w_ref, w_buf, *gather_refs)
-    run_ahead(w_buf, xs, slopes, scales, u_own)
+    run_ahead(w_buf, xs, slopes, scales, units)
+    u_own, dh_own = units.at[section], slants.at[section]
 
     def factor(ref, small, large):
         keep(small.part, 0, dot(ref[:, :HALF], ref[:, :HALF], (0, 0)))
@@ -459,7 +457,7 @@
         for t, at in ((1, 2), (2, 5)):
             pl.when(step == at)(functools.partial(advance, in_pair, t))
 
-    run_back(w_buf, xs, slopes, scales, grads, dh_own, beside_back)
+    run_back(w_buf, xs, slopes, scales, grads, slants, beside_back)
     factor(dh_own, g_small, g_large)
     advance(out_pair, 0)
     keep(d_top.part, 0, dot(u_own[:, :HALF], dh_own[...], (0, 0)))
@@ -499,7 +497,7 @@
         square(LAYERS + 1, jnp.bfloat16),
         square(LAYERS, jnp.float32),
         pltpu.VMEM((LAYERS, TOKENS, 128), jnp.float32),
-        flat(jnp.bfloat16), flat(jnp.bfloat16), flat(jnp.bfloat16),
+        flat(jnp.bfloat16), square(LAYERS, jnp.bfloat16), square(LAYERS, jnp.bfloat16),
         square(2, jnp.float32), flat(jnp.float32),
         pltpu.VMEM((8, HALF), jnp.float32),
         pltpu.VMEM((8, HALF), jnp.float32),

time: 141 us -> 138 us (0.979)
  Pallas kernels: 140 us -> 137 us
    pallas_call x1, Pallas kernels: 140 us -> 137 us  [local(): pl.pallas_call(kernel, out_shape=jax.ShapeDtypeStruct((8, WIDTH), jnp.flo...]
where the time goes in v5:
time: 138 us
  Pallas kernels  137 us (99%)
    pallas_call x1, Pallas kernels, local(): pl.pallas_call(kernel, out_shape=jax.ShapeDtypeStruct((8, WIDTH), jnp.flo...  137 us

profile of v5, /device:TPU:8, one launch (start us, length us, event | category | flops | bytes accessed | tf_op | source)
XLA Modules:
  0.0 137.9 jit_solution(332265564460371652)
XLA Ops:
  0.0 136.5 %chain_and_factors.1 = f32[8,512]{1,0:T(8,128)} custom-call(bf16[512,512]{1,0:T(8,128)(2,1)} %bitcast.2, bf16[512,512]{1,0:T(8,128)(2,1)} %bitcast.3, bf16[8,512]{1,0:T(8,128)(2,1)} %w_ref.1), custom_call_target="tpu_custom_call" | custom-call | tf_op jit(solution)/shard_map/chain_and_factors/pallas_call | solution.py:512
  136.6 1.3 copy.5

commit v6 on v5

--- a/solution.py
+++ b/solution.py
@@ -468,13 +468,12 @@
             advance(in_pair, t + 2)
         if t + 2 == 6:
             load_factor(mats, 0, a_small.full, a_large.full)
-        if t >= 2:
-            advance(d_pair, t - 2)
+        advance(d_pair, t - 1)
     load_factor(mats, 1, g_small.full, g_large.full)
 
     def beside_invert(step):
-        if step in (2, 4):
-            advance(d_pair, 4 + step // 2)
+        if step == 2:
+            advance(d_pair, 6)
 
     invert(mats, beside_invert)
     d_mat = jnp.concatenate([packed(d_top.full), packed(d_low.full)], axis=0)

time: 138 us -> 140 us (1.014)
    pallas_call x1, Pallas kernels: 137 us -> 138 us  [local(): pl.pallas_call(kernel, out_shape=jax.ShapeDtypeStruct((8, WIDTH), jnp.flo...]
where the time goes in v6:
time: 140 us
  Pallas kernels  138 us (99%)
    pallas_call x1, Pallas kernels, local(): pl.pallas_call(kernel, out_shape=jax.ShapeDtypeStruct((8, WIDTH), jnp.flo...  138 us

profile of v6, /device:TPU:8, one launch (start us, length us, event | category | flops | bytes accessed | tf_op | source)
XLA Modules:
  0.0 139.6 jit_solution(12555116847801727020)
XLA Ops:
  0.0 138.3 %chain_and_factors.1 = f32[8,512]{1,0:T(8,128)} custom-call(bf16[512,512]{1,0:T(8,128)(2,1)} %bitcast.2, bf16[512,512]{1,0:T(8,128)(2,1)} %bitcast.3, bf16[8,512]{1,0:T(8,128)(2,1)} %w_ref.1), custom_call_target="tpu_custom_call" | custom-call | tf_op jit(solution)/shard_map/chain_and_factors/pallas_call | solution.py:511
  138.3 1.3 copy.5
